TPU v7x, 128 devices: a whole 4x4x4 slice. The times are simulated.
128 devices in a mesh: seq: 32 (over z, x, core), head: 4 (over y).
Axes of the slice: x: 4, y: 4, z: 4, core: 2. Of those that a mesh axis runs over, the one named last changes fastest.
Arguments:
- queries: bfloat16 [65536, 2048], P('seq', 'head'), may hold values from -8 to 8
- key_rows: bfloat16 [65536, 2048], P('seq', 'head'), may hold values from -8 to 8
- value_rows: bfloat16 [65536, 2048], P('seq', 'head'), may hold values from -6 to 6
- cluster_ids: int32 [16, 65536, 1], P('head', 'seq'), may hold values from 0 to 255; in each aligned block of 2048 rows (0 to 2047, 2048 to 4095, ..., all dimensions but the last counted through in order) at most 12 rows name the same one
- centroids: float32 [16, 256, 128], P('head', 'seq'), may hold values from -6 to 6
- out_weight: bfloat16 [2048, 2048], P('head'), may hold values from -0.125 to 0.125
Outputs:
- mixed: bfloat16 [65536, 2048], P(('seq', 'head'))
- new_centroids: float32 [16, 256, 128], P('head', 'seq')
Inputs may be any that keep to these rules, and one draw needn't show every extreme that they name: `cluster_ids`: in each head and among the 2048 tokens of each index of seq, no cluster holds more than 12 tokens, and some cluster holds exactly 12.
All inputs are finite; a program needn't handle non-finite values.
Results may differ from a plain program's by a relative error of at most 0.0056.
Values may be sent and summed in bfloat16 or wider, within the bound.
A program may use at most 128 MiB of HBM per device.

v0:
```python
import math

import jax
import jax.numpy as jnp
from jax import lax
from jax.sharding import PartitionSpec as P

HD = 128
CLUSTERS = 256
CAP = 12
PRIOR = 8


def cluster_attention(packed, places):
    query_part = packed[..., :HD]
    key_part = packed[..., HD : 2 * HD]
    value_part = packed[..., 2 * HD :]
    score_scale = 1.0 / math.sqrt(HD)
    scores = (
        jnp.einsum("crd,csd->crs", query_part, key_part, preferred_element_type=jnp.float32)
        * score_scale
    )
    limit = jnp.where(places < 0, 1 << 30, places)
    allowed = (places[:, None, :] >= 0) & (places[:, None, :] <= limit[:, :, None])
    scores = jnp.where(allowed, scores, -1e30)
    row_max = jnp.max(scores, axis=-1, keepdims=True)
    raw_weights = jnp.exp(scores - row_max)
    weights = (raw_weights / jnp.sum(raw_weights, axis=-1, keepdims=True)).astype(jnp.bfloat16)
    return jnp.einsum(
        "crs,csd->crd", weights, value_part, preferred_element_type=jnp.float32
    ).astype(jnp.bfloat16)


def attend_item(item):
    return cluster_attention(item[0], item[1])


def shards(queries, key_rows, value_rows, cluster_ids, centroids, out_weight):
    token_count = queries.shape[0]
    head_local = centroids.shape[0]
    query_three = queries.reshape(token_count, head_local, HD)
    key_three = key_rows.reshape(token_count, head_local, HD)
    value_three = value_rows.reshape(token_count, head_local, HD)
    assigned = cluster_ids[:, :, 0]
    one_hot = (assigned[:, :, None] == jnp.arange(CLUSTERS, dtype=jnp.int32)).astype(jnp.bfloat16)
    block_count = token_count // 128
    blocks = one_hot.reshape(head_local, block_count, 128, CLUSTERS)
    counter = jnp.arange(128, dtype=jnp.int32)
    lower_mask = (counter[:, None] > counter[None, :]).astype(jnp.bfloat16)
    within = jnp.einsum("ij,hbjc->hbic", lower_mask, blocks, preferred_element_type=jnp.float32)
    totals = jnp.sum(blocks, axis=2, dtype=jnp.float32)
    offsets = jnp.cumsum(totals, axis=1) - totals
    ranks = jnp.sum((within + offsets[:, :, None, :]) * blocks, axis=-1)
    ranks = ranks.reshape(head_local, token_count).astype(jnp.int32)
    slot_by_token = (assigned * CAP + ranks).T
    head_grid = jnp.broadcast_to(
        jnp.arange(head_local, dtype=jnp.int32)[None, :], (token_count, head_local)
    )
    packed_rows = jnp.concatenate([query_three, key_three, value_three], axis=-1)
    send_rows = jnp.zeros((head_local, CLUSTERS * CAP, 3 * HD), jnp.bfloat16)
    send_rows = (
        send_rows.at[head_grid, slot_by_token]
        .set(packed_rows)
        .reshape(head_local, CLUSTERS, CAP, 3 * HD)
    )
    positions = lax.axis_index("seq") * token_count + jnp.arange(token_count, dtype=jnp.int32)
    send_places = jnp.full((head_local, CLUSTERS * CAP), -1, jnp.int32)
    send_places = send_places.at[head_grid, slot_by_token].set(
        jnp.broadcast_to(positions[:, None], (token_count, head_local))
    )
    send_places = send_places.reshape(head_local, CLUSTERS, CAP)
    received_rows = lax.all_to_all(send_rows, "seq", split_axis=1, concat_axis=2, tiled=True)
    received_places = lax.all_to_all(send_places, "seq", split_axis=1, concat_axis=2, tiled=True)
    attended_rows = lax.map(attend_item, (received_rows, received_places))
    returned_rows = lax.all_to_all(attended_rows, "seq", split_axis=2, concat_axis=1, tiled=True)
    outcome = returned_rows
    returned_rows = outcome
    local_sums = jnp.einsum("htc,thd->hcd", one_hot, key_three, preferred_element_type=jnp.float32)
    local_counts = jnp.sum(one_hot, axis=1, dtype=jnp.float32)
    key_sums, key_counts = (
        lax.psum_scatter(local_sums, "seq", scatter_dimension=1, tiled=True),
        lax.psum_scatter(local_counts, "seq", scatter_dimension=1, tiled=True),
    )
    flat_rows = returned_rows.reshape(head_local * CLUSTERS * CAP, HD)
    attended = flat_rows[head_grid * (CLUSTERS * CAP) + slot_by_token].reshape(
        token_count, head_local * HD
    )
    mixed = lax.psum_scatter(
        jnp.dot(attended, out_weight, preferred_element_type=jnp.float32),
        "head",
        scatter_dimension=0,
        tiled=True,
    )
    prior_weight = PRIOR
    new_centroids = (prior_weight * centroids + key_sums) / (prior_weight + key_counts)[..., None]
    return (mixed.astype(jnp.bfloat16), new_centroids)


def solution(mesh):
    placed = (
        P("seq", "head"),
        P("seq", "head"),
        P("seq", "head"),
        P("head", "seq", None),
        P("head", "seq", None),
        P("head", None),
    )
    return jax.shard_map(
        shards,
        mesh=mesh,
        in_specs=placed,
        out_specs=(P(("seq", "head"), None), P("head", "seq", None)),
        check_vma=False,
    )
```

profile of v0, /device:TPU:1, one launch (start us, length us, event | category | flops | bytes accessed | tf_op | source)
XLA Modules:
  0.0 615.4 jit_solution(2783397893107595966)
XLA Ops:
  7.2 2.3 convert_reduce_fusion
  9.6 4.1 fusion.41
  14.0 0.4 copy.22
  14.4 0.6 reshape.102
  15.0 0.3 broadcast_in_dim.60
  15.4 0.6 reshape.104
  16.0 30.5 %scatter_custom_fusion = s32[12288]{0:T(1024)S(1)} fusion(s32[8192]{0:T(1024)S(1)} %reshape.102, s32[8192]{0:T(1024)S(1)} %reshape.104, s32[]{:T(128)} %constant.12.clone.1), kind=kCustom, calls=%fused_computation.62 | custom fusion | bytes 49156
  46.5 0.6 reshape.77
  47.1 0.3 copy.71
  47.4 1.3 reshape.125
  48.7 9.7 %all-to-all-start = ((s32[32,1,384]{2,1,0:T(1,128)}), s32[32,1,384]{2,1,0:T(1,128)S(1)}, u32[]{:S(2)}, u32[]{:S(2)}) async-start(s32[32,1,384]{2,1,0:T(1,128)} %reshape.125), calls=%async_computation | async-start | bytes 98304 | tf_op jit(solution)/shard_map/all_to_all | solution.py:73
  58.4 4.0 reshape.78
  62.4 4.0 reshape.79
  66.4 4.0 reshape.80
  70.4 8.1 %pad_maximum_fusion = bf16[2048,4,384]{2,1,0:T(4,128)(2,1)} fusion(bf16[2048,4,128]{2,1,0:T(4,128)(2,1)} %reshape.80, bf16[2048,4,128]{2,1,0:T(4,128)(2,1)} %reshape.79, bf16[2048,4,128]{2,1,0:T(4,128)(2,1)} %reshape.78), kind=kLoop, calls=%fused_computation.42 | loop fusion | flops 18874368 | bytes 12582912 | tf_op jit(solution)/shard_map/concatenate | solution.py:59
  78.4 10.7 %reshape.110 = bf16[8192,384]{1,0:T(8,128)(2,1)} reshape(bf16[2048,4,384]{2,1,0:T(4,128)(2,1)} %pad_maximum_fusion) | data formatting | bytes 12582912 | tf_op jit(solution)/shard_map/concatenate | solution.py:59
  89.2 41.0 %scatter_custom_fusion.1 = bf16[12288,384]{1,0:T(8,128)(2,1)} fusion(s32[8192]{0:T(1024)S(1)} %reshape.102, bf16[8192,384]{1,0:T(8,128)(2,1)} %reshape.110, bf16[]{:T(256)} %constant.9.clone.1), kind=kCustom, calls=%fused_computation.43 | custom fusion | bytes 9437696
  130.2 15.7 %reshape.81 = bf16[4,256,12,384]{3,2,1,0:T(8,128)(2,1)} reshape(bf16[12288,384]{1,0:T(8,128)(2,1)} %scatter_custom_fusion.1) | data formatting | bytes 18874368 | tf_op jit(solution)/shard_map/reshape | solution.py:64
  145.9 13.1 %copy.26 = bf16[4,256,12,384]{3,0,2,1:T(4,128)(2,1)} copy(bf16[4,256,12,384]{3,2,1,0:T(8,128)(2,1)} %reshape.81) | data formatting | bytes 18874368 | tf_op jit(solution)/shard_map/reshape | solution.py:64
  159.0 7.8 %all-to-all-start.1 = ((bf16[4,256,12,384]{3,0,2,1:T(4,128)(2,1)}), bf16[4,256,12,384]{3,0,2,1:T(4,128)(2,1)}, u32[]{:S(2)}, u32[]{:S(2)}) async-start(bf16[4,256,12,384]{3,0,2,1:T(4,128)(2,1)} %copy.26), calls=%async_computation.1 | async-start | bytes 18874368 | tf_op jit(solution)/shard_map/all_to_all | solution.py:72
  166.8 0.5 broadcast.106
  167.4 0.8 reduce.6
  168.1 0.7 reshape.126
  169.4 110.1 %all-to-all-done.1 = bf16[4,256,12,384]{3,0,2,1:T(4,128)(2,1)} async-done(((bf16[4,256,12,384]{3,0,2,1:T(4,128)(2,1)}), bf16[4,256,12,384]{3,0,2,1:T(4,128)(2,1)}, u32[]{:S(2)}, u32[]{:S(2)}) %all-to-all-start.1) | async-done | bytes 9437216 | tf_op jit(solution)/shard_map/all_to_all | solution.py:72
  279.5 9.8 %copy.68 = bf16[4,256,12,384]{3,1,2,0:T(8,128)(2,1)} copy(bf16[4,256,12,384]{3,0,2,1:T(4,128)(2,1)} %all-to-all-done.1) | data formatting | bytes 18874368 | tf_op jit(solution)/shard_map/all_to_all | solution.py:72
  289.3 8.4 %copy.28 = bf16[4,8,32,12,384]{4,1,3,2,0:T(8,128)(2,1)} copy(bf16[4,8,32,12,384]{4,1,2,3,0:T(8,128)(2,1)} %bitcast.80) | data formatting | bytes 18874368 | tf_op jit(solution)/shard_map/all_to_all | solution.py:72
  297.7 52.1 %while.10 = (s32[]{:T(128)}, bf16[4,8,384,128]{3,1,0,2:T(8,128)(2,1)}, s32[4,8,384]{2,1,0:T(8,128)S(1)}, bf16[4,8,384,384]{3,1,2,0:T(8,128)(2,1)}, s32[]{:T(128)}) while((s32[]{:T(128)}, bf16[4,8,384,128]{3,1,0,2:T(8,128)(2,1)}, s32[4,8,384]{2,1,0:T(8,128)S(1)}, bf16[4,8,384,384]{3,1,2,0:T(8,128)(2,1)}, s32[]{:T(128)}) %tuple.35), condition=%wide.region_8.9_spmd, body=%wide.region_5.8_spmd.sunk | while | flops 921711360 | bytes 15861317 | solution.py:74
  297.7 1.9 constant_dynamic-slice_fusion.2
  299.6 1.7 copy.75
  301.3 3.3 fusion.79
  304.6 4.6 fusion.80
  309.2 1.4 copy_dynamic-update-slice_fusion.2
  310.7 1.9 constant_dynamic-slice_fusion.2
  312.6 1.7 copy.75
  314.3 3.3 fusion.79
  317.6 4.6 fusion.80
  322.2 1.5 copy_dynamic-update-slice_fusion.2
  323.7 1.9 constant_dynamic-slice_fusion.2
  325.6 1.7 copy.75
  327.3 3.3 fusion.79
  330.6 4.6 fusion.80
  335.2 1.5 copy_dynamic-update-slice_fusion.2
  336.7 1.9 constant_dynamic-slice_fusion.2
  338.6 1.7 copy.75
  340.3 3.3 fusion.79
  343.7 4.6 fusion.80
  348.3 1.5 copy_dynamic-update-slice_fusion.2
  349.8 11.1 %all-to-all-start.2 = ((bf16[4,8,384,128]{3,1,0,2:T(8,128)(2,1)}), bf16[4,8,384,128]{3,1,0,2:T(8,128)(2,1)}, u32[]{:S(2)}, u32[]{:S(2)}) async-start(bf16[4,8,384,128]{3,1,0,2:T(8,128)(2,1)} %get-tuple-element.24), calls=%async_computation.2 | async-start | bytes 6291456 | tf_op jit(solution)/shard_map/all_to_all | solution.py:75
  360.9 3.7 fusion.43
  364.9 0.4 copy.33
  365.3 0.6 reshape.96
  365.9 34.2 %all-to-all-done.2 = bf16[4,8,384,128]{3,1,0,2:T(8,128)(2,1)} async-done(((bf16[4,8,384,128]{3,1,0,2:T(8,128)(2,1)}), bf16[4,8,384,128]{3,1,0,2:T(8,128)(2,1)}, u32[]{:S(2)}, u32[]{:S(2)}) %all-to-all-start.2) | async-done | bytes 3145760 | tf_op jit(solution)/shard_map/all_to_all | solution.py:75
  400.2 6.0 copy.32
  406.2 6.3 %reshape.82 = bf16[12288,128]{1,0:T(8,128)(2,1)} reshape(bf16[4,32,8,12,128]{4,3,2,1,0:T(8,128)(2,1)} %copy.32) | data formatting | bytes 6291456 | tf_op jit(solution)/shard_map/reshape | solution.py:84
  412.5 30.5 %gather_fusion = bf16[8192,128]{1,0:T(8,128)(2,1)} fusion(bf16[12288,128]{1,0:T(8,128)(2,1)} %reshape.82, s32[8192]{0:T(1024)S(1)} %broadcast_clamp_fusion), kind=kCustom, calls=%fused_computation | custom fusion | bytes 4227072 | tf_op jit(solution)/shard_map/gather | solution.py:85
  443.0 4.4 reshape.83
  447.4 9.6 %fusion.63 = f32[2048,2048]{1,0:T(8,128)} fusion(bf16[2048,512]{1,0:T(8,128)(2,1)} %reshape.83, bf16[512,2048]{1,0:T(8,128)(2,1)S(1)} %copy-done), kind=kOutput, calls=%fused_computation.72 | convolution fusion | flops 4294967296 | bytes 20971520 | tf_op jit(solution)/shard_map/dot_general | solution.py:89
  457.0 0.6 copy-done.5
  457.7 0.6 dynamic-slice
  458.9 0.9 convert_reduce_fusion.1
  459.8 64.9 %all-reduce = f32[4,256]{1,0:T(4,128)S(1)} all-reduce(f32[4,256]{1,0:T(4,128)S(1)} %convert_reduce_fusion.1), channel_id=4, replica_groups=mesh['seq'=32,'head'=4] {'seq'}, use_global_device_ids=true, to_apply=%region_12.13.clone | all-reduce | flops 1024 | bytes 8192
  524.8 1.4 add_divide_fusion
  526.2 78.1 %reduce-scatter.4.cloned.1.call-done = f32[512,2048]{1,0:T(8,128)} async-done(((f32[2048,2048]{1,0:T(8,128)}), f32[512,2048]{1,0:T(8,128)}) %reduce-scatter.4.cloned.1.call-update) | async-done | bytes 4194320 | tf_op jit(solution)/shard_map/reduce_scatter | solution.py:88
  604.3 3.8 convert_element_type.33
  (41 shorter events, 1.5 us)
Async XLA Ops:
  7.2 440.2 %copy-start = (bf16[512,2048]{1,0:T(8,128)(2,1)S(1)}, bf16[512,2048]{1,0:T(8,128)(2,1)}, u32[]{:S(2)}) copy-start(bf16[512,2048]{1,0:T(8,128)(2,1)} %param.13) | copy-start | bytes 6291460
  9.6 4.1 copy-start.1
  9.6 4.2 copy-start.4
  9.6 4.3 copy-start.3
  48.7 110.3 %all-to-all-start = ((s32[32,1,384]{2,1,0:T(1,128)}), s32[32,1,384]{2,1,0:T(1,128)S(1)}, u32[]{:S(2)}, u32[]{:S(2)}) async-start(s32[32,1,384]{2,1,0:T(1,128)} %reshape.125), calls=%async_computation | async-start | bytes 98304 | tf_op jit(solution)/shard_map/all_to_all | solution.py:73
  159.0 120.5 %all-to-all-start.1 = ((bf16[4,256,12,384]{3,0,2,1:T(4,128)(2,1)}), bf16[4,256,12,384]{3,0,2,1:T(4,128)(2,1)}, u32[]{:S(2)}, u32[]{:S(2)}) async-start(bf16[4,256,12,384]{3,0,2,1:T(4,128)(2,1)} %copy.26), calls=%async_computation.1 | async-start | bytes 18874368 | tf_op jit(solution)/shard_map/all_to_all | solution.py:72
  349.8 50.4 %all-to-all-start.2 = ((bf16[4,8,384,128]{3,1,0,2:T(8,128)(2,1)}), bf16[4,8,384,128]{3,1,0,2:T(8,128)(2,1)}, u32[]{:S(2)}, u32[]{:S(2)}) async-start(bf16[4,8,384,128]{3,1,0,2:T(8,128)(2,1)} %get-tuple-element.24), calls=%async_computation.2 | async-start | bytes 6291456 | tf_op jit(solution)/shard_map/all_to_all | solution.py:75
  360.9 163.9 %reduce-scatter.6.cloned.1.call-start = ((), (), s32[]{:S(2)}) async-start(), calls=%async_computation.6 | async-start | bytes 540672 | tf_op jit(solution)/shard_map/reduce_scatter | solution.py:81
  364.6 239.7 %reduce-scatter.4.cloned.1.call-start = ((), (), s32[]{:S(2)}) async-start(), calls=%async_computation.5 | async-start | bytes 20971520 | tf_op jit(solution)/shard_map/reduce_scatter | solution.py:88
  457.0 0.7 copy-start.5
  457.0 67.8 %copy-start.2 = (f32[4,8,128]{2,1,0:T(8,128)S(1)}, f32[4,8,128]{2,1,0:T(8,128)}, u32[]{:S(2)}) copy-start(f32[4,8,128]{2,1,0:T(8,128)} %param.12) | copy-start | bytes 49156
Sparse Core Ops, SparseCore 0:
  365.2 76.5 reduce-scatter.5
  457.2 147.0 reduce-scatter.3
where the time goes:
time: 623 us; the launch traced here: 615 us
  waiting for transfers between devices  223 us (36%)
  local copies, waits for them, and re-layouts  217 us (35%)
  blocking collectives  64.9 us (10%)
  matrix products  49 us (8%)
  starting transfers between devices  29 us (5%)
  other arithmetic  17.8 us (3%)
  between operations  15.4 us (2%)
    all_to_all x1, waiting for transfers between devices, shards(): lax.all_to_all(send_rows, 'seq', split_axis=1, concat_axis=2, tiled=True)  110 us
    reduce_scatter x1, waiting for transfers between devices, shards(): lax.psum_scatter(jnp.dot(attended, out_weight, preferred_element_type=jnp...  78.1 us
    unnamed x20, local copies, waits for them, and re-layouts  75.7 us
    unnamed x1, blocking collectives  64.9 us
    all_to_all x1, waiting for transfers between devices, shards(): lax.all_to_all(attended_rows, 'seq', split_axis=2, concat_axis=1, tiled=T...  34.2 us
    gather x1, local copies, waits for them, and re-layouts, shards(): flat_rows[head_grid * (CLUSTERS * CAP) + slot_by_token]  30.5 us
    reshape x2, local copies, waits for them, and re-layouts, shards(): send_rows = send_rows.at[head_grid, slot_by_token].set(packed_rows).resha...  28.8 us
    dot_general x4, matrix products, cluster_attention(): jnp.einsum('crs,csd->crd', weights, value_part, preferred_element_type=jn...  18.3 us
  transfers between devices with their start and end apart: 5, of which 3 were waited for; matrix products, arithmetic and copies ran while one was open for 27% of the time, Pallas kernels for 0%

commit v1 on v0

v1 whole, which is shorter than its diff:
```python
import functools
import math

import jax
import jax.numpy as jnp
import numpy as np
from jax import lax
from jax.experimental import pallas as pl
from jax.experimental.pallas import tpu as pltpu
from jax.sharding import PartitionSpec as P

HD = 128
CLUSTERS = 256
CAP = 12
PRIOR = 8.0
N_SEQ = 32
N_HEAD = 4
OWN = CLUSTERS // N_SEQ
CHUNK = OWN * CAP
TOK = 2048
HEADS = 4
GROUP = 4
ROWS = GROUP * CHUNK
MEMBERS = N_SEQ * CAP
BLOCK = 128
TBLOCK = TOK // N_HEAD
MARK = 64.0
NEG = -1e30
MESH = pl.DeviceIdType.MESH
BF = jnp.bfloat16
F32 = jnp.float32
ORDER = (0, 1, 2, 6, 3, 7, 8, 24, 9, 25, 4, 5, 10, 30, 11, 31, 14, 26, 15, 27, 16, 17, 12, 28, 13, 29, 18, 22, 19, 23, 20, 21)


def rearrangement():
    src, clu, rank = np.meshgrid(np.arange(GROUP), np.arange(OWN), np.arange(CAP), indexing="ij")
    matrix = np.zeros((ROWS, ROWS), np.float32)
    matrix[(clu * GROUP * CAP + src * CAP + rank).ravel(), (src * CHUNK + clu * CAP + rank).ravel()] = 1
    return matrix


def kernel(
    q_ref, k_ref, v_ref, ids_ref, cent_ref, w_ref, perm_ref, back_ref,
    out_ref, nc_ref,
    x_ref, base_ref, p_ref, send, recv, aq, ak, av, oarr, rsend, rrecv, lo_ref, pt_ref, atok, ytok, wall, acc,
    xsem, qs, qr, rs, rr, ys, yr, ws, wr, wl,
):
    me = lax.axis_index("seq")
    hh = lax.axis_index("head")
    z, x, core = me // 8, (me // 2) % 4, me % 2

    def peer(k):
        dz, dx, dc = k // 8, (k // 2) % 4, k % 2
        a = dz + core * (dx - dz)
        b = dx + core * (dz - dx)
        return ((z + a) % 4) * 8 + ((x + b) % 4) * 2 + (core + dc) % 2

    def loads(h, slot):
        cols = pl.ds(pl.multiple_of(h * HD, HD), HD)
        return [
            pltpu.make_async_copy(ref.at[:, cols], x_ref.at[slot, :, pl.ds(i * HD, HD)], xsem.at[slot, i])
            for i, ref in enumerate((q_ref, k_ref, v_ref))
        ]

    barrier = pltpu.get_barrier_semaphore()

    @pl.loop(1, N_SEQ)
    def _(k):
        pl.semaphore_signal(barrier, inc=1, device_id=(peer(k), hh), device_id_type=MESH)

    @pl.loop(1, N_HEAD)
    def _(k):
        pl.semaphore_signal(barrier, inc=1, device_id=(me, (hh + k) % N_HEAD), device_id_type=MESH)

    for slot in range(2):
        for copy in loads(slot, slot):
            copy.start()
    own_weight = pltpu.make_async_copy(w_ref, wall.at[:, hh], wl)
    own_weight.start()

    lane0 = lax.broadcasted_iota(jnp.int32, (TOK, HD), 1) == 0
    x_ref[0, :, 3 * HD :] = jnp.where(lane0, MARK, 0.0).astype(BF)
    x_ref[1, :, 3 * HD :] = jnp.where(lane0, MARK, 0.0).astype(BF)
    first = (lax.broadcasted_iota(jnp.int32, (16, HD), 0) == 0) & (lax.broadcasted_iota(jnp.int32, (16, HD), 1) == 0)
    for c in range(OWN):
        aq[c, MEMBERS : MEMBERS + 16, :] = jnp.where(first, 1.0, 0.0).astype(BF)

    pl.semaphore_wait(barrier, N_SEQ - 1 + N_HEAD - 1)

    @pl.loop(1, N_HEAD)
    def _(k):
        pltpu.make_async_remote_copy(
            w_ref, wall.at[:, hh], ws, wr, device_id=(me, (hh + k) % N_HEAD), device_id_type=MESH
        ).start()

    @pl.loop(0, HEADS)
    def _(h):
        slot = h % 2
        before = jnp.where(
            lax.broadcasted_iota(jnp.int32, (256, 256), 0) < lax.broadcasted_iota(jnp.int32, (256, 256), 1), 1.0, 0.0
        ).astype(BF)
        cluster = lax.broadcasted_iota(jnp.int32, (CLUSTERS, 256), 0)
        sofar = jnp.zeros((CLUSTERS, 1), F32)
        row96 = lax.broadcasted_iota(jnp.int32, (CHUNK, 256), 0)
        lane = lax.broadcasted_iota(jnp.int32, (256, 128), 1)
        for b in range(TOK // 256):
            cols = slice(256 * b, 256 * b + 256)
            named = ids_ref[pl.ds(h, 1), cols]
            hot = jnp.where(cluster == named, 1.0, 0.0)
            earlier = jnp.dot(hot.astype(BF), before, preferred_element_type=F32)
            rank = jnp.sum(hot * (earlier + sofar), axis=0, keepdims=True).astype(jnp.int32)
            sofar = sofar + jnp.sum(hot, axis=1, keepdims=True)
            within = (named & 7) * CAP + rank
            owner = (named >> 3).astype(F32)
            base_ref[:, cols] = jnp.where(row96 == within, owner, -1.0).astype(BF)
            place = jnp.broadcast_to((named * CAP + rank).astype(F32), (128, 256)).T.astype(jnp.int32)
            lo_ref[h, cols, :] = jnp.where((place & 127) == lane, (place >> 7).astype(F32), -1.0).astype(BF)
        for copy in loads(h, slot):
            copy.wait()
        mark = jnp.where(lax.broadcasted_iota(jnp.int32, (ROWS, HD), 1) == 0, MARK, 0.0)
        for j in range(N_SEQ // GROUP):
            targets = [peer(k) for k in ORDER[GROUP * j : GROUP * j + GROUP]]
            for i, target in enumerate(targets):
                p_ref[CHUNK * i : CHUNK * i + CHUNK, :] = jnp.where(
                    base_ref[...] == target.astype(F32).astype(BF), 1.0, 0.0
                ).astype(BF)
            rows = jnp.dot(p_ref[...], x_ref[slot], preferred_element_type=F32)
            keys = rows[:, HD : 2 * HD] + (mark - rows[:, 3 * HD :])
            rows = jnp.concatenate([rows[:, :HD], keys, rows[:, 2 * HD : 3 * HD]], axis=1).astype(BF)
            rows = rows.reshape(GROUP, CHUNK, 3 * HD)
            send[h, GROUP * j : GROUP * j + GROUP] = rows
            for i, target in enumerate(targets):
                if GROUP * j + i == 0:
                    recv[h, me] = rows[0]
                else:
                    pltpu.make_async_remote_copy(
                        send.at[h, GROUP * j + i], recv.at[h, me], qs.at[h], qr.at[h],
                        device_id=(target, hh), device_id_type=MESH,
                    ).start()

        @pl.when(h < HEADS - 2)
        def _():
            for copy in loads(h + 2, slot):
                copy.start()

    def arrivals(h):
        others = pl.ds(0, N_SEQ - 1)
        return pltpu.make_async_remote_copy(
            send.at[h, others], recv.at[h, others], qs.at[h], qr.at[h], device_id=(me, hh), device_id_type=MESH
        )

    def returns(h):
        others = pl.ds(0, N_SEQ - 1)
        return pltpu.make_async_remote_copy(
            rsend.at[h, others], rrecv.at[h, others], rs.at[h], rr.at[h], device_id=(me, hh), device_id_type=MESH
        )

    def exchanged(h):
        return pltpu.make_async_remote_copy(
            atok.at[h, pl.ds(0, N_HEAD - 1)], ytok.at[h, :, pl.ds(0, (N_HEAD - 1) * HD)], ys.at[h], yr.at[h],
            device_id=(me, hh), device_id_type=MESH,
        )

    @pl.loop(0, HEADS)
    def _(h):
        arrivals(h).wait_recv()

        @pl.loop(0, N_SEQ // GROUP)
        def _(g):
            piece = recv[h, pl.ds(g * GROUP, GROUP)].reshape(ROWS, 3 * HD)
            moved = jnp.dot(perm_ref[...], piece, preferred_element_type=F32).astype(BF)
            for c in range(OWN):
                part = moved[48 * c : 48 * c + 48]
                where = pl.ds(pl.multiple_of(g * 48, 16), 48)
                aq[c, where, :] = part[:, :HD]
                ak[c, where, :] = part[:, HD : 2 * HD]
                av[c, where, :] = part[:, 2 * HD :]

        factor = math.log2(math.e) / math.sqrt(HD)

        @pl.loop(0, OWN)
        def _(c):
            keys = ak[c]
            values = av[c]
            causal = jnp.where(
                lax.broadcasted_iota(jnp.int32, (BLOCK, BLOCK), 1) <= lax.broadcasted_iota(jnp.int32, (BLOCK, BLOCK), 0),
                0.0, NEG,
            )
            bias = None
            for r in (2, 1, 0):
                width = BLOCK * (r + 1)
                rows = aq[c, BLOCK * r : (MEMBERS + 16 if r == 2 else BLOCK * (r + 1)), :]
                scores = lax.dot_general(
                    rows, keys[:width], (((1,), (1,)), ((), ())), preferred_element_type=F32
                )
                if r == 2:
                    present = jnp.where(scores[BLOCK : BLOCK + 1, :] < MARK / 2, 1.0, 0.0)
                    bias = jnp.where(present > 0.5, 0.0, NEG)
                    present8 = jnp.broadcast_to(present, (8, MEMBERS))
                    sums = jnp.dot(present8.astype(BF), keys, preferred_element_type=F32)[0:1]
                    count = jnp.sum(present, axis=1, keepdims=True)
                    nc_ref[h, pl.ds(c, 1), :] = (PRIOR * cent_ref[h, pl.ds(c, 1), :] + sums) / (PRIOR + count)
                    scores = scores[:BLOCK]
                scores = scores * factor + bias[:, :width]
                last = scores[:, width - BLOCK :] + causal
                scores = last if r == 0 else jnp.concatenate([scores[:, : width - BLOCK], last], axis=1)
                top = jnp.max(scores, axis=1, keepdims=True)
                raw = jnp.exp2(scores - top)
                weights = (raw / jnp.sum(raw, axis=1, keepdims=True)).astype(BF)
                oarr[c, BLOCK * r : BLOCK * r + BLOCK, :] = jnp.dot(
                    weights, values[:width], preferred_element_type=F32
                ).astype(BF)

        @pl.loop(0, N_SEQ // GROUP)
        def _(g):
            piece = oarr[:, pl.ds(pl.multiple_of(g * 48, 16), 48), :].reshape(ROWS, HD)
            moved = jnp.dot(back_ref[...], piece, preferred_element_type=F32).astype(BF)
            rsend[h, pl.ds(g * GROUP, GROUP)] = moved.reshape(GROUP, CHUNK, HD)

        rrecv[h, me] = rsend[h, me]
        for k in ORDER[1:]:
            target = peer(k)
            pltpu.make_async_remote_copy(
                rsend.at[h, target], rrecv.at[h, me], rs.at[h], rr.at[h],
                device_id=(target, hh), device_id_type=MESH,
            ).start()

    own_weight.wait()
    pltpu.make_async_remote_copy(
        wall.at[:, pl.ds(0, N_HEAD - 1)], wall.at[:, pl.ds(0, N_HEAD - 1)], ws, wr,
        device_id=(me, hh), device_id_type=MESH,
    ).wait_recv()

    def project(h):
        exchanged(h).wait_recv()
        for n in range(4):
            cols = slice(512 * n, 512 * n + 512)
            part = jnp.dot(
                ytok[h], wall[h, :, :, cols].reshape(N_HEAD * HD, 512), preferred_element_type=F32
            )
            acc[:, cols] = acc[:, cols] + part

    acc[...] = jnp.zeros_like(acc)

    @pl.loop(0, HEADS)
    def _(h):
        returns(h).wait_recv()

        @pl.loop(1, N_HEAD + 1)
        def _(k):
            to = (hh + k) % N_HEAD
            known = lo_ref[h, pl.ds(pl.multiple_of(to * TBLOCK, TBLOCK), TBLOCK), :]
            for j in range(CLUSTERS * CAP // 128):
                pt_ref[:, 128 * j : 128 * j + 128] = jnp.where(known == float(j), 1.0, 0.0).astype(BF)
            rows = jnp.dot(
                pt_ref[...], rrecv[h].reshape(CLUSTERS * CAP, HD), preferred_element_type=F32
            ).astype(BF)
            atok[h, to] = rows

            @pl.when(k < N_HEAD)
            def _():
                pltpu.make_async_remote_copy(
                    atok.at[h, to], ytok.at[h, :, pl.ds(pl.multiple_of(hh * HD, HD), HD)], ys.at[h], yr.at[h],
                    device_id=(me, to), device_id_type=MESH,
                ).start()

        ytok[h, :, pl.ds(pl.multiple_of(hh * HD, HD), HD)] = atok[h, hh]

        @pl.when(h > 0)
        def _():
            project(h - 1)

    project(HEADS - 1)
    out_ref[...] = acc[...].astype(BF)

    @pl.loop(0, HEADS)
    def _(h):
        arrivals(h).wait_send()
        returns(h).wait_send()
        exchanged(h).wait_send()

    pltpu.make_async_remote_copy(
        wall.at[:, pl.ds(0, N_HEAD - 1)], wall.at[:, pl.ds(0, N_HEAD - 1)], ws, wr,
        device_id=(me, hh), device_id_type=MESH,
    ).wait_send()


def shards(queries, key_rows, value_rows, cluster_ids, centroids, out_weight):
    perm = rearrangement()
    hbm = pl.BlockSpec(memory_space=pl.ANY)
    vmem = pl.BlockSpec(memory_space=pltpu.VMEM)
    return pl.pallas_call(
        kernel,
        out_shape=(
            jax.ShapeDtypeStruct((TBLOCK, 2048), BF),
            jax.ShapeDtypeStruct((HEADS, OWN, HD), F32),
        ),
        in_specs=[hbm, hbm, hbm, vmem, vmem, hbm, vmem, vmem],
        out_specs=(vmem, vmem),
        scratch_shapes=[
            pltpu.VMEM((2, TOK, 4 * HD), BF),
            pltpu.VMEM((CHUNK, TOK), BF),
            pltpu.VMEM((ROWS, TOK), BF),
            pltpu.VMEM((HEADS, N_SEQ, CHUNK, 3 * HD), BF),
            pltpu.VMEM((HEADS, N_SEQ, CHUNK, 3 * HD), BF),
            pltpu.VMEM((OWN, MEMBERS + 16, HD), BF),
            pltpu.VMEM((OWN, MEMBERS, HD), BF),
            pltpu.VMEM((OWN, MEMBERS, HD), BF),
            pltpu.VMEM((OWN, MEMBERS, HD), BF),
            pltpu.VMEM((HEADS, N_SEQ, CHUNK, HD), BF),
            pltpu.VMEM((HEADS, N_SEQ, CHUNK, HD), BF),
            pltpu.VMEM((HEADS, TOK, HD), BF),
            pltpu.VMEM((TBLOCK, CLUSTERS * CAP), BF),
            pltpu.VMEM((HEADS, N_HEAD, TBLOCK, HD), BF),
            pltpu.VMEM((HEADS, TBLOCK, N_HEAD * HD), BF),
            pltpu.VMEM((HEADS, N_HEAD, HD, 2048), BF),
            pltpu.VMEM((TBLOCK, 2048), F32),
            pltpu.SemaphoreType.DMA((2, 3)),
            pltpu.SemaphoreType.DMA((HEADS,)),
            pltpu.SemaphoreType.DMA((HEADS,)),
            pltpu.SemaphoreType.DMA((HEADS,)),
            pltpu.SemaphoreType.DMA((HEADS,)),
            pltpu.SemaphoreType.DMA((HEADS,)),
            pltpu.SemaphoreType.DMA((HEADS,)),
            pltpu.SemaphoreType.DMA,
            pltpu.SemaphoreType.DMA,
            pltpu.SemaphoreType.DMA,
        ],
        compiler_params=pltpu.CompilerParams(
            collective_id=0, has_side_effects=True, vmem_limit_bytes=63 << 20
        ),
    )(
        queries, key_rows, value_rows, cluster_ids.reshape(HEADS, TOK), centroids,
        out_weight.reshape(HEADS, HD, 2048),
        jnp.asarray(perm, BF), jnp.asarray(perm.T, BF),
    )


def solution(mesh):
    placed = (
        P("seq", "head"),
        P("seq", "head"),
        P("seq", "head"),
        P("head", "seq", None),
        P("head", "seq", None),
        P("head", None),
    )
    return jax.shard_map(
        shards,
        mesh=mesh,
        in_specs=placed,
        out_specs=(P(("seq", "head"), None), P("head", "seq", None)),
        check_vma=False,
    )
```

time: 623 us -> 181 us (0.29); the launches traced: 615 us -> 180 us
  waiting for transfers between devices: 223 us -> 0 us
  local copies, waits for them, and re-layouts: 217 us -> 5.16 us
  Pallas kernels: 0 us -> 175 us
  blocking collectives: 64.9 us -> 0 us
  matrix products: 49 us -> 0 us
  starting transfers between devices: 29 us -> 0 us
  other arithmetic: 17.8 us -> 0 us
  between operations: 15.4 us -> 0.65 us
    pallas_call x0 -> x1, Pallas kernels: none -> 175 us  [shards(): pl.pallas_call(kernel, out_shape=(jax.ShapeDtypeStruct((TBLOCK, 2048), BF...]
    all_to_all x3 -> x0, waiting for transfers between devices: 144 us -> none  [the longest x1 110 us: shards(): lax.all_to_all(send_rows, 'seq', split_axis=1, concat_axis=2, tiled=True)]
    reduce_scatter x2 -> x0, waiting for transfers between devices: 78.1 us -> none  [the longest x1 78.1 us: shards(): lax.psum_scatter(jnp.dot(attended, out_weight, preferred_element_type=jnp...]
    unnamed x20 -> x5, local copies, waits for them, and re-layouts: 75.7 us -> 5.16 us
    unnamed x1 -> x0, blocking collectives: 64.9 us -> none
    reshape x9 -> x0, local copies, waits for them, and re-layouts: 52.3 us -> none  [the longest x2 28.8 us: shards(): send_rows = send_rows.at[head_grid, slot_by_token].set(packed_rows).resha...]
    dot_general x7 -> x0, matrix products: 35.6 us -> none  [the longest x4 18.3 us: cluster_attention(): jnp.einsum('crs,csd->crd', weights, value_part, preferred_element_type=jn...]
    gather x1 -> x0, local copies, waits for them, and re-layouts: 30.5 us -> none  [shards(): flat_rows[head_grid * (CLUSTERS * CAP) + slot_by_token]]
  transfers between devices with their start and end apart: 5 -> 0, of which waited for: 3 -> 0; matrix products, arithmetic and copies ran while one was open for 27% -> 0% of each run, Pallas kernels for 0% -> 0%
where the time goes in v1:
time: 181 us; the launch traced here: 180 us
  Pallas kernels  175 us (97%)
  local copies, waits for them, and re-layouts  5.16 us (3%)
    pallas_call x1, Pallas kernels, shards(): pl.pallas_call(kernel, out_shape=(jax.ShapeDtypeStruct((TBLOCK, 2048), BF...  175 us
    unnamed x5, local copies, waits for them, and re-layouts  5.16 us

profile of v1, /device:TPU:1, one launch (start us, length us, event | category | flops | bytes accessed | tf_op | source)
XLA Modules:
  0.0 180.4 jit_solution(4412131533846651419)
XLA Ops:
  0.6 1.4 copy.12
  2.0 174.5 %shard_map.95 = (bf16[512,2048]{1,0:T(8,128)(2,1)}, f32[4,8,128]{2,1,0:T(8,128)}) custom-call(bf16[2048,512]{1,0:T(8,128)(2,1)} %q_ref.1, bf16[2048,512]{1,0:T(8,128)(2,1)} %k_ref.1, bf16[2048,512]{1,0:T(8,128)(2,1)} %v_ref.1, s32[4,2048]{1,0:T(4,128)} %bitcast.5, f32[4,8,128]{2,1,0:T(8,128)} %cent_ref.1, bf16[4,128,2048]{2,1,0:T(8,128)(2,1)} %bitcast.4, ...), custom_call_target="tpu_custom_call" | custom-call | tf_op jit(solution)/shard_map/pallas_call | solution.py:292
  176.6 0.0 copy-start
  176.6 3.2 %copy.15 = bf16[512,2048]{1,0:T(8,128)(2,1)} copy(bf16[512,2048]{1,0:T(8,128)(2,1)} %get-tuple-element.4) | data formatting | bytes 4194304
  179.7 0.0 copy-done
  179.7 0.6 copy.16
Async XLA Ops:
  176.6 3.2 %copy-start = (f32[4,8,128]{2,1,0:T(8,128)S(1)}, f32[4,8,128]{2,1,0:T(8,128)}, u32[]{:S(2)}) copy-start(f32[4,8,128]{2,1,0:T(8,128)} %get-tuple-element.5) | copy-start | bytes 49156

commit v2 on v1

--- a/solution.py
+++ b/solution.py
@@ -30,6 +30,13 @@
 BF = jnp.bfloat16
 F32 = jnp.float32
 ORDER = (0, 1, 2, 6, 3, 7, 8, 24, 9, 25, 4, 5, 10, 30, 11, 31, 14, 26, 15, 27, 16, 17, 12, 28, 13, 29, 18, 22, 19, 23, 20, 21)
+TABLE = tuple(
+    (
+        sum(k // 8 * 4**n for n, k in enumerate(ORDER[place::4])),
+        sum(k % 8 * 8**n for n, k in enumerate(ORDER[place::4])),
+    )
+    for place in range(4)
+)
 
 
 def rearrangement():
@@ -41,19 +48,30 @@
 
 def kernel(
     q_ref, k_ref, v_ref, ids_ref, cent_ref, w_ref, perm_ref, back_ref,
-    out_ref, nc_ref,
-    x_ref, base_ref, p_ref, send, recv, aq, ak, av, oarr, rsend, rrecv, lo_ref, pt_ref, atok, ytok, wall, acc,
-    xsem, qs, qr, rs, rr, ys, yr, ws, wr, wl,
+    acc_out, y_last, w_last, nc_ref,
+    x_ref, base_ref, p_ref, pt_ref, send, recv, aq, ak, av, oarr, rsend, rrecv, lo_ref, atok, ytok, wall, acc,
+    xsem, qs, qr, rs, rr, ys, yr, ws, wr, wl, os,
 ):
     me = lax.axis_index("seq")
     hh = lax.axis_index("head")
     z, x, core = me // 8, (me // 2) % 4, me % 2
 
-    def peer(k):
-        dz, dx, dc = k // 8, (k // 2) % 4, k % 2
+    def device_at(dz, dx, dc):
         a = dz + core * (dx - dz)
         b = dx + core * (dz - dx)
         return ((z + a) % 4) * 8 + ((x + b) % 4) * 2 + (core + dc) % 2
+
+    def peer(k):
+        return device_at(k // 8, (k // 2) % 4, k % 2)
+
+    def four(table):
+        return [device_at(far % 4, (near // 2) % 4, near % 2) for far, near in table]
+
+    def shifted(table):
+        return tuple((far // 4, near // 8) for far, near in table)
+
+    def tables():
+        return tuple((jnp.int32(far), jnp.int32(near)) for far, near in TABLE)
 
     def loads(h, slot):
         cols = pl.ds(pl.multiple_of(h * HD, HD), HD)
@@ -84,14 +102,6 @@
     first = (lax.broadcasted_iota(jnp.int32, (16, HD), 0) == 0) & (lax.broadcasted_iota(jnp.int32, (16, HD), 1) == 0)
     for c in range(OWN):
         aq[c, MEMBERS : MEMBERS + 16, :] = jnp.where(first, 1.0, 0.0).astype(BF)
-
-    pl.semaphore_wait(barrier, N_SEQ - 1 + N_HEAD - 1)
-
-    @pl.loop(1, N_HEAD)
-    def _(k):
-        pltpu.make_async_remote_copy(
-            w_ref, wall.at[:, hh], ws, wr, device_id=(me, (hh + k) % N_HEAD), device_id_type=MESH
-        ).start()
 
     @pl.loop(0, HEADS)
     def _(h):
@@ -103,9 +113,10 @@
         sofar = jnp.zeros((CLUSTERS, 1), F32)
         row96 = lax.broadcasted_iota(jnp.int32, (CHUNK, 256), 0)
         lane = lax.broadcasted_iota(jnp.int32, (256, 128), 1)
+        named16 = ids_ref[pl.ds(pl.multiple_of(h * 16, 16), 16), :]
         for b in range(TOK // 256):
             cols = slice(256 * b, 256 * b + 256)
-            named = ids_ref[pl.ds(h, 1), cols]
+            named = jnp.concatenate([named16[2 * b : 2 * b + 1], named16[2 * b + 1 : 2 * b + 2]], axis=1)
             hot = jnp.where(cluster == named, 1.0, 0.0)
             earlier = jnp.dot(hot.astype(BF), before, preferred_element_type=F32)
             rank = jnp.sum(hot * (earlier + sofar), axis=0, keepdims=True).astype(jnp.int32)
@@ -115,11 +126,13 @@
             base_ref[:, cols] = jnp.where(row96 == within, owner, -1.0).astype(BF)
             place = jnp.broadcast_to((named * CAP + rank).astype(F32), (128, 256)).T.astype(jnp.int32)
             lo_ref[h, cols, :] = jnp.where((place & 127) == lane, (place >> 7).astype(F32), -1.0).astype(BF)
+        mark = jnp.where(lax.broadcasted_iota(jnp.int32, (ROWS, HD), 1) == 0, MARK, 0.0)
+
         for copy in loads(h, slot):
             copy.wait()
-        mark = jnp.where(lax.broadcasted_iota(jnp.int32, (ROWS, HD), 1) == 0, MARK, 0.0)
-        for j in range(N_SEQ // GROUP):
-            targets = [peer(k) for k in ORDER[GROUP * j : GROUP * j + GROUP]]
+
+        def pack(j, table):
+            targets = four(table)
             for i, target in enumerate(targets):
                 p_ref[CHUNK * i : CHUNK * i + CHUNK, :] = jnp.where(
                     base_ref[...] == target.astype(F32).astype(BF), 1.0, 0.0
@@ -128,15 +141,37 @@
             keys = rows[:, HD : 2 * HD] + (mark - rows[:, 3 * HD :])
             rows = jnp.concatenate([rows[:, :HD], keys, rows[:, 2 * HD : 3 * HD]], axis=1).astype(BF)
             rows = rows.reshape(GROUP, CHUNK, 3 * HD)
-            send[h, GROUP * j : GROUP * j + GROUP] = rows
-            for i, target in enumerate(targets):
-                if GROUP * j + i == 0:
-                    recv[h, me] = rows[0]
-                else:
+            send[h, pl.ds(GROUP * j, GROUP)] = rows
+
+            @pl.when(j == 0)
+            def _():
+                recv[h, me] = rows[0]
+
+            @pl.when((h == 0) & (j == 0))
+            def _():
+                pl.semaphore_wait(barrier, N_SEQ - 1 + N_HEAD - 1)
+
+            def ship(i):
+                pltpu.make_async_remote_copy(
+                    send.at[h, GROUP * j + i], recv.at[h, me], qs.at[h], qr.at[h],
+                    device_id=(targets[i], hh), device_id_type=MESH,
+                ).start()
+
+            pl.when(j > 0)(functools.partial(ship, 0))
+            for i in range(1, GROUP):
+                ship(i)
+
+            @pl.when((h == 0) & (j == 0))
+            def _():
+                @pl.loop(1, N_HEAD)
+                def _(k):
                     pltpu.make_async_remote_copy(
-                        send.at[h, GROUP * j + i], recv.at[h, me], qs.at[h], qr.at[h],
-                        device_id=(target, hh), device_id_type=MESH,
+                        w_ref, wall.at[:, hh], ws, wr, device_id=(me, (hh + k) % N_HEAD), device_id_type=MESH
                     ).start()
+
+            return shifted(table)
+
+        lax.fori_loop(0, N_SEQ // GROUP, pack, tables())
 
         @pl.when(h < HEADS - 2)
         def _():
@@ -155,9 +190,12 @@
             rsend.at[h, others], rrecv.at[h, others], rs.at[h], rr.at[h], device_id=(me, hh), device_id_type=MESH
         )
 
+    def landing(h, where):
+        return y_last.at[:, where] if isinstance(h, int) else ytok.at[h, :, where]
+
     def exchanged(h):
         return pltpu.make_async_remote_copy(
-            atok.at[h, pl.ds(0, N_HEAD - 1)], ytok.at[h, :, pl.ds(0, (N_HEAD - 1) * HD)], ys.at[h], yr.at[h],
+            atok.at[h, pl.ds(0, N_HEAD - 1)], landing(h, pl.ds(0, (N_HEAD - 1) * HD)), ys.at[h], yr.at[h],
             device_id=(me, hh), device_id_type=MESH,
         )
 
@@ -178,8 +216,7 @@
 
         factor = math.log2(math.e) / math.sqrt(HD)
 
-        @pl.loop(0, OWN)
-        def _(c):
+        def attend(c):
             keys = ak[c]
             values = av[c]
             causal = jnp.where(
@@ -206,10 +243,12 @@
                 scores = last if r == 0 else jnp.concatenate([scores[:, : width - BLOCK], last], axis=1)
                 top = jnp.max(scores, axis=1, keepdims=True)
                 raw = jnp.exp2(scores - top)
-                weights = (raw / jnp.sum(raw, axis=1, keepdims=True)).astype(BF)
+                weights = (raw * (1.0 / jnp.sum(raw, axis=1, keepdims=True))).astype(BF)
                 oarr[c, BLOCK * r : BLOCK * r + BLOCK, :] = jnp.dot(
                     weights, values[:width], preferred_element_type=F32
                 ).astype(BF)
+
+        pl.loop(0, OWN)(attend)
 
         @pl.loop(0, N_SEQ // GROUP)
         def _(g):
@@ -218,18 +257,31 @@
             rsend[h, pl.ds(g * GROUP, GROUP)] = moved.reshape(GROUP, CHUNK, HD)
 
         rrecv[h, me] = rsend[h, me]
-        for k in ORDER[1:]:
-            target = peer(k)
-            pltpu.make_async_remote_copy(
-                rsend.at[h, target], rrecv.at[h, me], rs.at[h], rr.at[h],
-                device_id=(target, hh), device_id_type=MESH,
-            ).start()
+
+        def give(j, table):
+            targets = four(table)
+
+            def ship(i):
+                pltpu.make_async_remote_copy(
+                    rsend.at[h, targets[i]], rrecv.at[h, me], rs.at[h], rr.at[h],
+                    device_id=(targets[i], hh), device_id_type=MESH,
+                ).start()
+
+            pl.when(j > 0)(functools.partial(ship, 0))
+            for i in range(1, GROUP):
+                ship(i)
+            return shifted(table)
+
+        lax.fori_loop(0, N_SEQ // GROUP, give, tables())
 
     own_weight.wait()
-    pltpu.make_async_remote_copy(
+    weights_in = pltpu.make_async_remote_copy(
         wall.at[:, pl.ds(0, N_HEAD - 1)], wall.at[:, pl.ds(0, N_HEAD - 1)], ws, wr,
         device_id=(me, hh), device_id_type=MESH,
-    ).wait_recv()
+    )
+    weights_in.wait_recv()
+    last_weight = pltpu.make_async_copy(wall.at[HEADS - 1], w_last, os.at[0])
+    last_weight.start()
 
     def project(h):
         exchanged(h).wait_recv()
@@ -240,10 +292,9 @@
             )
             acc[:, cols] = acc[:, cols] + part
 
-    acc[...] = jnp.zeros_like(acc)
-
-    @pl.loop(0, HEADS)
-    def _(h):
+    mine = pl.ds(pl.multiple_of(hh * HD, HD), HD)
+
+    def restore(h):
         returns(h).wait_recv()
 
         @pl.loop(1, N_HEAD + 1)
@@ -252,55 +303,79 @@
             known = lo_ref[h, pl.ds(pl.multiple_of(to * TBLOCK, TBLOCK), TBLOCK), :]
             for j in range(CLUSTERS * CAP // 128):
                 pt_ref[:, 128 * j : 128 * j + 128] = jnp.where(known == float(j), 1.0, 0.0).astype(BF)
-            rows = jnp.dot(
+            atok[h, to] = jnp.dot(
                 pt_ref[...], rrecv[h].reshape(CLUSTERS * CAP, HD), preferred_element_type=F32
             ).astype(BF)
-            atok[h, to] = rows
 
             @pl.when(k < N_HEAD)
             def _():
                 pltpu.make_async_remote_copy(
-                    atok.at[h, to], ytok.at[h, :, pl.ds(pl.multiple_of(hh * HD, HD), HD)], ys.at[h], yr.at[h],
-                    device_id=(me, to), device_id_type=MESH,
+                    atok.at[h, to], landing(h, mine), ys.at[h], yr.at[h], device_id=(me, to), device_id_type=MESH
                 ).start()
 
-        ytok[h, :, pl.ds(pl.multiple_of(hh * HD, HD), HD)] = atok[h, hh]
+    acc[...] = jnp.zeros_like(acc)
+
+    @pl.loop(0, HEADS - 1)
+    def _(h):
+        restore(h)
+        ytok[h, :, mine] = atok[h, hh]
 
         @pl.when(h > 0)
         def _():
             project(h - 1)
 
-    project(HEADS - 1)
-    out_ref[...] = acc[...].astype(BF)
+    restore(HEADS - 1)
+    own_last = pltpu.make_async_copy(atok.at[HEADS - 1, hh], y_last.at[:, mine], os.at[1])
+    own_last.start()
+
+    @pl.loop(HEADS - 2, HEADS - 1)
+    def _(h):
+        project(h)
+
+    total = pltpu.make_async_copy(acc, acc_out, os.at[2])
+    total.start()
+    exchanged(HEADS - 1).wait_recv()
+    own_last.wait()
+    last_weight.wait()
+    total.wait()
 
     @pl.loop(0, HEADS)
     def _(h):
         arrivals(h).wait_send()
         returns(h).wait_send()
+
+    @pl.loop(0, HEADS - 1)
+    def _(h):
         exchanged(h).wait_send()
 
-    pltpu.make_async_remote_copy(
-        wall.at[:, pl.ds(0, N_HEAD - 1)], wall.at[:, pl.ds(0, N_HEAD - 1)], ws, wr,
-        device_id=(me, hh), device_id_type=MESH,
-    ).wait_send()
+    exchanged(HEADS - 1).wait_send()
+    weights_in.wait_send()
+
+
+def finish(acc_ref, y_ref, w_ref, nc_in, out_ref, nc_out):
+    out_ref[...] = (acc_ref[...] + jnp.dot(y_ref[...], w_ref[...], preferred_element_type=F32)).astype(BF)
+    nc_out[...] = nc_in[...]
 
 
 def shards(queries, key_rows, value_rows, cluster_ids, centroids, out_weight):
     perm = rearrangement()
     hbm = pl.BlockSpec(memory_space=pl.ANY)
     vmem = pl.BlockSpec(memory_space=pltpu.VMEM)
-    return pl.pallas_call(
+    total, y_last, w_last, centers = pl.pallas_call(
         kernel,
         out_shape=(
-            jax.ShapeDtypeStruct((TBLOCK, 2048), BF),
+            jax.ShapeDtypeStruct((TBLOCK, 2048), F32),
+            jax.ShapeDtypeStruct((TBLOCK, N_HEAD * HD), BF),
+            jax.ShapeDtypeStruct((N_HEAD, HD, 2048), BF),
             jax.ShapeDtypeStruct((HEADS, OWN, HD), F32),
         ),
         in_specs=[hbm, hbm, hbm, vmem, vmem, hbm, vmem, vmem],
-        out_specs=(vmem, vmem),
+        out_specs=(hbm, hbm, hbm, vmem),
         scratch_shapes=[
             pltpu.VMEM((2, TOK, 4 * HD), BF),
             pltpu.VMEM((CHUNK, TOK), BF),
             pltpu.VMEM((ROWS, TOK), BF),
+            pltpu.VMEM((TBLOCK, CLUSTERS * CAP), BF),
             pltpu.VMEM((HEADS, N_SEQ, CHUNK, 3 * HD), BF),
             pltpu.VMEM((HEADS, N_SEQ, CHUNK, 3 * HD), BF),
             pltpu.VMEM((OWN, MEMBERS + 16, HD), BF),
@@ -310,9 +385,8 @@
             pltpu.VMEM((HEADS, N_SEQ, CHUNK, HD), BF),
             pltpu.VMEM((HEADS, N_SEQ, CHUNK, HD), BF),
             pltpu.VMEM((HEADS, TOK, HD), BF),
-            pltpu.VMEM((TBLOCK, CLUSTERS * CAP), BF),
             pltpu.VMEM((HEADS, N_HEAD, TBLOCK, HD), BF),
-            pltpu.VMEM((HEADS, TBLOCK, N_HEAD * HD), BF),
+            pltpu.VMEM((HEADS - 1, TBLOCK, N_HEAD * HD), BF),
             pltpu.VMEM((HEADS, N_HEAD, HD, 2048), BF),
             pltpu.VMEM((TBLOCK, 2048), F32),
             pltpu.SemaphoreType.DMA((2, 3)),
@@ -325,15 +399,35 @@
             pltpu.SemaphoreType.DMA,
             pltpu.SemaphoreType.DMA,
             pltpu.SemaphoreType.DMA,
+            pltpu.SemaphoreType.DMA((3,)),
         ],
         compiler_params=pltpu.CompilerParams(
             collective_id=0, has_side_effects=True, vmem_limit_bytes=63 << 20
         ),
     )(
-        queries, key_rows, value_rows, cluster_ids.reshape(HEADS, TOK), centroids,
+        queries, key_rows, value_rows, cluster_ids.reshape(HEADS * TOK // 128, 128), centroids,
         out_weight.reshape(HEADS, HD, 2048),
         jnp.asarray(perm, BF), jnp.asarray(perm.T, BF),
     )
+    tile = 512
+    return pl.pallas_call(
+        finish,
+        grid=(2048 // tile,),
+        out_shape=(
+            jax.ShapeDtypeStruct((TBLOCK, 2048), BF),
+            jax.ShapeDtypeStruct((HEADS, OWN, HD), F32),
+        ),
+        in_specs=[
+            pl.BlockSpec((TBLOCK, tile), lambda n: (0, n)),
+            pl.BlockSpec((TBLOCK, N_HEAD * HD), lambda n: (0, 0)),
+            pl.BlockSpec((N_HEAD * HD, tile), lambda n: (0, n)),
+            pl.BlockSpec((HEADS, OWN, HD), lambda n: (0, 0, 0)),
+        ],
+        out_specs=(
+            pl.BlockSpec((TBLOCK, tile), lambda n: (0, n)),
+            pl.BlockSpec((HEADS, OWN, HD), lambda n: (0, 0, 0)),
+        ),
+    )(total, y_last, w_last.reshape(N_HEAD * HD, 2048), centers)
 
 
 def solution(mesh):

time: 181 us -> 179 us (0.989)
  local copies, waits for them, and re-layouts: 5.16 us -> 0 us
  Pallas kernels: 175 us -> 177 us
    unnamed x5 -> x0, local copies, waits for them, and re-layouts: 5.16 us -> none
    pallas_call x1 -> x2, Pallas kernels: 175 us -> 177 us  [the longest x1 171 us: shards(): pl.pallas_call(kernel, out_shape=(jax.ShapeDtypeStruct((TBLOCK, 2048), F3...]
where the time goes in v2:
time: 179 us; the launch traced here: 178 us
  Pallas kernels  177 us (99%)
    pallas_call x1, Pallas kernels, shards(): pl.pallas_call(kernel, out_shape=(jax.ShapeDtypeStruct((TBLOCK, 2048), F3...  171 us
    pallas_call x1, Pallas kernels, shards(): pl.pallas_call(finish, grid=(2048 // tile,), out_shape=(jax.ShapeDtypeStr...  5.57 us

profile of v2, /device:TPU:1, one launch (start us, length us, event | category | flops | bytes accessed | tf_op | source)
XLA Modules:
  0.0 177.7 jit_solution(6662317047069235096)
XLA Ops:
  0.6 171.5 %shard_map.95 = (f32[512,2048]{1,0:T(8,128)}, bf16[512,512]{1,0:T(8,128)(2,1)}, bf16[4,128,2048]{2,1,0:T(8,128)(2,1)}, f32[4,8,128]{2,1,0:T(8,128)}) custom-call(bf16[2048,512]{1,0:T(8,128)(2,1)} %q_ref.1, bf16[2048,512]{1,0:T(8,128)(2,1)} %k_ref.1, bf16[2048,512]{1,0:T(8,128)(2,1)} %v_ref.1, s32[64,128]{1,0:T(8,128)} %bitcast.5, f32[4,8,128]{2,1,0:T(8,128)} %cent_ref.1, ...), custom_call_target="tpu_custom_call" | custom-call | tf_op jit(solution)/shard_map/pallas_call | solution.py:364
  172.1 5.6 %shard_map.96 = (bf16[512,2048]{1,0:T(8,128)(2,1)}, f32[4,8,128]{2,1,0:T(8,128)}) custom-call(f32[512,2048]{1,0:T(8,128)} %get-tuple-element.6.acc_ref, bf16[512,512]{1,0:T(8,128)(2,1)} %get-tuple-element.7.y_ref, bf16[512,2048]{1,0:T(8,128)(2,1)} %bitcast.4, f32[4,8,128]{2,1,0:T(8,128)} %get-tuple-element.9.nc_in), custom_call_target="tpu_custom_call" | custom-call | tf_op jit(solution)/shard_map/pallas_call | solution.py:413

commit v3 on v2

--- a/solution.py
+++ b/solution.py
@@ -46,6 +46,11 @@
     return matrix
 
 
+def one_where(held, wanted):
+    apart = held - wanted
+    return jnp.maximum(BF(1) - apart * apart, BF(0))
+
+
 def kernel(
     q_ref, k_ref, v_ref, ids_ref, cent_ref, w_ref, perm_ref, back_ref,
     acc_out, y_last, w_last, nc_ref,
@@ -134,9 +139,7 @@
         def pack(j, table):
             targets = four(table)
             for i, target in enumerate(targets):
-                p_ref[CHUNK * i : CHUNK * i + CHUNK, :] = jnp.where(
-                    base_ref[...] == target.astype(F32).astype(BF), 1.0, 0.0
-                ).astype(BF)
+                p_ref[CHUNK * i : CHUNK * i + CHUNK, :] = one_where(base_ref[...], target.astype(F32).astype(BF))
             rows = jnp.dot(p_ref[...], x_ref[slot], preferred_element_type=F32)
             keys = rows[:, HD : 2 * HD] + (mark - rows[:, 3 * HD :])
             rows = jnp.concatenate([rows[:, :HD], keys, rows[:, 2 * HD : 3 * HD]], axis=1).astype(BF)
@@ -302,7 +305,7 @@
             to = (hh + k) % N_HEAD
             known = lo_ref[h, pl.ds(pl.multiple_of(to * TBLOCK, TBLOCK), TBLOCK), :]
             for j in range(CLUSTERS * CAP // 128):
-                pt_ref[:, 128 * j : 128 * j + 128] = jnp.where(known == float(j), 1.0, 0.0).astype(BF)
+                pt_ref[:, 128 * j : 128 * j + 128] = one_where(known, BF(j))
             atok[h, to] = jnp.dot(
                 pt_ref[...], rrecv[h].reshape(CLUSTERS * CAP, HD), preferred_element_type=F32
             ).astype(BF)

time: 179 us -> 169 us (0.944)
  Pallas kernels: 177 us -> 166 us
    pallas_call x1, Pallas kernels: 171 us -> 161 us  [shards(): pl.pallas_call(kernel, out_shape=(jax.ShapeDtypeStruct((TBLOCK, 2048), F3...]
where the time goes in v3:
time: 169 us; the launch traced here: 167 us
  Pallas kernels  166 us (98%)
    pallas_call x1, Pallas kernels, shards(): pl.pallas_call(kernel, out_shape=(jax.ShapeDtypeStruct((TBLOCK, 2048), F3...  161 us
    pallas_call x1, Pallas kernels, shards(): pl.pallas_call(finish, grid=(2048 // tile,), out_shape=(jax.ShapeDtypeStr...  5.57 us

profile of v3, /device:TPU:1, one launch (start us, length us, event | category | flops | bytes accessed | tf_op | source)
XLA Modules:
  0.0 166.9 jit_solution(15934569408685694544)
XLA Ops:
  0.6 160.7 %shard_map.95 = (f32[512,2048]{1,0:T(8,128)}, bf16[512,512]{1,0:T(8,128)(2,1)}, bf16[4,128,2048]{2,1,0:T(8,128)(2,1)}, f32[4,8,128]{2,1,0:T(8,128)}) custom-call(bf16[2048,512]{1,0:T(8,128)(2,1)} %q_ref.1, bf16[2048,512]{1,0:T(8,128)(2,1)} %k_ref.1, bf16[2048,512]{1,0:T(8,128)(2,1)} %v_ref.1, s32[64,128]{1,0:T(8,128)} %bitcast.5, f32[4,8,128]{2,1,0:T(8,128)} %cent_ref.1, ...), custom_call_target="tpu_custom_call" | custom-call | tf_op jit(solution)/shard_map/pallas_call | solution.py:367
  161.4 5.6 %shard_map.96 = (bf16[512,2048]{1,0:T(8,128)(2,1)}, f32[4,8,128]{2,1,0:T(8,128)}) custom-call(f32[512,2048]{1,0:T(8,128)} %get-tuple-element.6.acc_ref, bf16[512,512]{1,0:T(8,128)(2,1)} %get-tuple-element.7.y_ref, bf16[512,2048]{1,0:T(8,128)(2,1)} %bitcast.4, f32[4,8,128]{2,1,0:T(8,128)} %get-tuple-element.9.nc_in), custom_call_target="tpu_custom_call" | custom-call | tf_op jit(solution)/shard_map/pallas_call | solution.py:416

commit v4 on v3

--- a/solution.py
+++ b/solution.py
@@ -301,7 +301,9 @@
         returns(h).wait_recv()
 
         @pl.loop(1, N_HEAD + 1)
-        def _(k):
+        def _(n):
+            late = n // 3
+            k = late * n + (1 - late) * (3 - n)
             to = (hh + k) % N_HEAD
             known = lo_ref[h, pl.ds(pl.multiple_of(to * TBLOCK, TBLOCK), TBLOCK), :]
             for j in range(CLUSTERS * CAP // 128):
@@ -412,7 +414,7 @@
         out_weight.reshape(HEADS, HD, 2048),
         jnp.asarray(perm, BF), jnp.asarray(perm.T, BF),
     )
-    tile = 512
+    tile = 1024
     return pl.pallas_call(
         finish,
         grid=(2048 // tile,),

time: 169 us -> 167 us (0.988); the launches traced: 167 us -> 167 us
  no operation moved by 1% of the time
where the time goes in v4:
time: 167 us
  Pallas kernels  166 us (99%)
    pallas_call x1, Pallas kernels, shards(): pl.pallas_call(kernel, out_shape=(jax.ShapeDtypeStruct((TBLOCK, 2048), F3...  161 us
    pallas_call x1, Pallas kernels, shards(): pl.pallas_call(finish, grid=(2048 // tile,), out_shape=(jax.ShapeDtypeStr...  4.67 us

profile of v4, /device:TPU:1, one launch (start us, length us, event | category | flops | bytes accessed | tf_op | source)
XLA Modules:
  0.0 166.7 jit_solution(16445371112523616209)
XLA Ops:
  0.6 161.4 %shard_map.95 = (f32[512,2048]{1,0:T(8,128)}, bf16[512,512]{1,0:T(8,128)(2,1)}, bf16[4,128,2048]{2,1,0:T(8,128)(2,1)}, f32[4,8,128]{2,1,0:T(8,128)}) custom-call(bf16[2048,512]{1,0:T(8,128)(2,1)} %q_ref.1, bf16[2048,512]{1,0:T(8,128)(2,1)} %k_ref.1, bf16[2048,512]{1,0:T(8,128)(2,1)} %v_ref.1, s32[64,128]{1,0:T(8,128)} %bitcast.5, f32[4,8,128]{2,1,0:T(8,128)} %cent_ref.1, ...), custom_call_target="tpu_custom_call" | custom-call | tf_op jit(solution)/shard_map/pallas_call | solution.py:369
  162.0 4.7 %shard_map.96 = (bf16[512,2048]{1,0:T(8,128)(2,1)}, f32[4,8,128]{2,1,0:T(8,128)}) custom-call(f32[512,2048]{1,0:T(8,128)} %get-tuple-element.6.acc_ref, bf16[512,512]{1,0:T(8,128)(2,1)} %get-tuple-element.7.y_ref, bf16[512,2048]{1,0:T(8,128)(2,1)} %bitcast.4, f32[4,8,128]{2,1,0:T(8,128)} %get-tuple-element.9.nc_in), custom_call_target="tpu_custom_call" | custom-call | tf_op jit(solution)/shard_map/pallas_call | solution.py:418
